TPU v7x, 256 devices: a whole 4x4x8 slice. The times are simulated.
256 devices in a mesh: seq: 32 (over z, y), head: 8 (over x, core).
Axes of the slice: x: 4, y: 4, z: 8, core: 2. Of those that a mesh axis runs over, the one named last changes fastest.
Arguments:
- q_data: bfloat16 [32768, 6144], P(('seq', 'head')), may hold values from -20 to 20
- k_data: bfloat16 [32768, 6144], P(('seq', 'head')), may hold values from -20 to 20
- v_data: bfloat16 [32768, 6144], P(('seq', 'head')), may hold values from -6 to 6
- q_exp: int32 [256, 48], P(('seq', 'head')), may hold values from -1 to 1
- k_exp: int32 [256, 48], P(('seq', 'head')), may hold values from -1 to 1
- v_exp: int32 [256, 48], P(('seq', 'head')), may hold values from -1 to 1
- extents: int32 [48, 3], replicated, may hold values from 0 to 3, as said below
Outputs:
- attended: bfloat16 [32768, 6144], P(('seq', 'head'))
Inputs may be any that keep to these rules, and one draw needn't show every extreme that they name: `extents`: column 0 is 0 or 1, column 1 at most 3, column 2 at most 1; some head has all three largest values.
All inputs are finite; a program needn't handle non-finite values.
Results may differ from a plain program's by a relative error of at most 0.0049.
Values may be sent and summed in bfloat16 or wider, within the bound.
A program may use at most 128 MiB of HBM per device.

v0:
```python
import functools
import math

import jax
import jax.numpy as jnp
from jax import lax
from jax.experimental import pallas as pl
from jax.experimental.pallas import tpu as pltpu
from jax.sharding import PartitionSpec as P

H = 48
HD = 128
TILE = 128
HT = 4
WT = 2
TILES = HT * WT
HALF = TILES // 2
FRAMES = 3
NEG = -1e30
LOG2_SCALE = math.log2(math.e) / math.sqrt(HD)
MESH = pl.DeviceIdType.MESH

PLANS = ((9, 3), (10, 3), (11, 3), (12, 6))
ROW_HEADS = 12
ROW_REACH = 8

SLOTS = H // TILES
ENTRIES = HT * HT + WT + FRAMES
ROW_TABLE = SLOTS * ENTRIES
ROW_ENTRIES = WT + FRAMES
TABLE = ROW_TABLE + ROW_HEADS * ROW_ENTRIES


def bytes_of(ref, sem):
    return pltpu.make_async_copy(ref, ref, sem)


def block_max(s):
    return jnp.max(s.reshape(s.shape[0] // 8, 8, s.shape[1]), axis=0)


def attend(q_ref, kv_ref, score_refs, write, table, slot, first_frame):
    frames = kv_ref.shape[0]
    entry = slot * ENTRIES

    def biases(row):
        rows = [table[entry + row * HT + r] for r in range(HT)]
        columns = [table[entry + HT * HT + c] for c in range(WT)]
        beside = [table[entry + HT * HT + WT + first_frame + f] for f in range(frames)]
        return lambda f, t, u: rows[t // WT] + columns[abs(t % WT - u)] + beside[f]

    def score(row, s_ref):
        bias = biases(row)
        queries = q_ref[pl.ds(row * WT, WT)].reshape(WT * TILE, HD)
        peak = [None] * WT
        for f in range(frames):
            for t in range(0, TILES, WT):
                keys = kv_ref[f, t : t + WT, 0].reshape(WT * TILE, HD)
                s = lax.dot_general(
                    keys, queries, (((1,), (1,)), ((), ())), preferred_element_type=jnp.float32
                )
                base = (f * TILES + t) * TILE
                s_ref[base : base + WT * TILE, :] = s
                for j in range(WT):
                    for u in range(WT):
                        block = s[j * TILE : (j + 1) * TILE, u * TILE : (u + 1) * TILE]
                        top = block_max(block) + bias(f, t + j, u)
                        peak[u] = top if peak[u] is None else jnp.maximum(peak[u], top)
        return [jnp.max(p, axis=0, keepdims=True) * LOG2_SCALE for p in peak]

    def combine(row, s_ref, peak):
        bias = biases(row)
        ones = jnp.ones((16, WT * TILE), jnp.bfloat16)
        total = None
        for f in range(frames):
            for t in range(0, TILES, WT):
                base = (f * TILES + t) * TILE
                columns = []
                for u in range(WT):
                    parts = []
                    for j in range(WT):
                        s = s_ref[base + j * TILE : base + (j + 1) * TILE, u * TILE : (u + 1) * TILE]
                        shift = bias(f, t + j, u) - peak[u]
                        parts.append(jnp.exp2(s * LOG2_SCALE + shift).astype(jnp.bfloat16))
                    columns.append(jnp.concatenate(parts, axis=0))
                weights = jnp.concatenate(columns, axis=1)
                values = jnp.concatenate([kv_ref[f, t + j, 1] for j in range(WT)], axis=1)
                values = jnp.concatenate([values, ones], axis=0)
                part = jnp.dot(values, weights, preferred_element_type=jnp.float32)
                total = part if total is None else total + part
        out = total[:HD] * (1.0 / total[HD : HD + 1])
        for u in range(WT):
            write(row * WT + u, out[:, u * TILE : (u + 1) * TILE].T.astype(jnp.bfloat16))

    def rows(i, carry):
        at = [i * 2 + j for j in range(2)]
        peaks = [score(r, s_ref) for r, s_ref in zip(at, score_refs)]
        for r, s_ref, peak in zip(at, score_refs, peaks):
            combine(r, s_ref, peak)
        return carry

    lax.fori_loop(0, HT // 2, rows, 0)


def attend_row(queries, kv_ref, frames, head, table):
    entry = ROW_TABLE + head * ROW_ENTRIES
    columns = [table[entry + c] for c in range(WT)]
    blocks = [(f, c, columns[c] + table[entry + WT + f]) for f in frames for c in range(WT)]
    scores = []
    peak = None
    for f, c, bias in blocks:
        s = lax.dot_general(
            kv_ref[f, c, head, 0], queries, (((1,), (1,)), ((), ())), preferred_element_type=jnp.float32
        )
        scores.append(s)
        top = block_max(s) + bias
        peak = top if peak is None else jnp.maximum(peak, top)
    peak = jnp.max(peak, axis=0, keepdims=True) * LOG2_SCALE
    weights = jnp.concatenate(
        [jnp.exp2(s * LOG2_SCALE + (bias - peak)) for s, (_, _, bias) in zip(scores, blocks)], axis=0
    ).astype(jnp.bfloat16)
    values = jnp.concatenate([kv_ref[f, c, head, 1] for f, c, _ in blocks], axis=1)
    values = jnp.concatenate([values, jnp.ones((16, values.shape[1]), jnp.bfloat16)], axis=0)
    total = jnp.dot(values, weights, preferred_element_type=jnp.float32)
    return (total[:HD] * (1.0 / total[HD : HD + 1])).T.astype(jnp.bfloat16)


def exchange_kernel(
    halves, wide, frame_total,
    table, kv_stage, q_stage,
    out,
    kv_wide, kv_near, kv_row, q_near, q_row, o_stage, o_row, scores_a, scores_b,
    kv_send, kv_recv, q_send, q_recv, halo_send, halo_recv, o_send, o_recv, own_sem,
    row_send, row_recv, side_send, side_recv, row_sem,
):
    full, half = halves // 2, halves % 2
    slots = full + half
    row_base = halves * HALF
    row_heads = H - row_base
    me = lax.axis_index("head")
    seq = lax.axis_index("seq")
    later = lax.rem(seq + 1, frame_total)
    earlier = lax.rem(seq + frame_total - 1, frame_total)
    column = lax.rem(me, WT)
    chip = me // WT
    sibling = me + 1 - 2 * column
    spot = column * HALF + chip

    def peer(d):
        return lax.rem(me + d, TILES)

    barrier = pltpu.get_barrier_semaphore()
    for d in range(1, TILES):
        pl.semaphore_signal(barrier, inc=1, device_id=(seq, peer(d)), device_id_type=MESH)
    for frame in (later, earlier):
        pl.semaphore_signal(barrier, inc=1, device_id=(frame, me), device_id_type=MESH)
    pl.semaphore_wait(barrier, TILES - 1 + 2)

    def remote(src, dst, send, recv, frame, group):
        return pltpu.make_async_remote_copy(
            src_ref=src, dst_ref=dst, send_sem=send, recv_sem=recv,
            device_id=(frame, group), device_id_type=MESH,
        )

    def wide_tile(s, t):
        return kv_wide.at[s, 1, t]

    def near_tile(s, t):
        return kv_near.at[s - wide, 0, t]

    def send_kv_tile(s, place, tile_at, group):
        src = kv_stage.at[s * TILES + place]
        remote(src, tile_at(s, me), kv_send.at[s], kv_recv.at[s], seq, group).start()

    def send_q_tile(s, place, group):
        src = q_stage.at[s * TILES + place]
        remote(src, q_near.at[s, me], q_send.at[s], q_recv.at[s], seq, group).start()

    def own_kv(s, tile_at):
        return pltpu.make_async_copy(kv_stage.at[s * TILES + spot], tile_at(s, me), own_sem.at[0, s])

    def own_q(s):
        return pltpu.make_async_copy(q_stage.at[s * TILES + spot], q_near.at[s, me], own_sem.at[1, s])

    def place_of(group):
        return lax.rem(group, WT) * HALF + group // WT

    def send_kv(s, tile_at):
        for d in range(1, TILES):
            group = peer(d)
            send_kv_tile(s, place_of(group), tile_at, group)
        own_kv(s, tile_at).start()

    def send_q(s):
        for d in range(1, TILES):
            group = peer(d)
            send_q_tile(s, place_of(group), group)
        own_q(s).start()

    def send_half(s):
        for i in range(1, HALF):
            place = lax.rem(chip + i, HALF)
            send_kv_tile(s, place, near_tile, place * WT)
        for i in range(1, HALF):
            place = lax.rem(chip + i, HALF)
            send_q_tile(s, place, place * WT)

        @pl.when(column == 0)
        def _():
            own_kv(s, near_tile).start()
            own_q(s).start()

        @pl.when(column == 1)
        def _():
            send_kv_tile(s, chip, near_tile, sibling)
            send_q_tile(s, chip, sibling)

    def halo_copies(s):
        return [
            remote(
                kv_wide.at[s, 1], kv_wide.at[s, 2 * side],
                halo_send.at[s, side], halo_recv.at[s, side], frame, me,
            )
            for side, frame in enumerate((later, earlier))
        ]

    row_parts = row_heads // HALF
    reach_parts = min(row_parts, 2)

    def part_of(f, part):
        return kv_row.at[f, column, pl.ds(part * HALF, HALF)]

    def staged_part(part):
        return kv_stage.at[pl.ds(row_base + part * HALF, HALF)]

    def row_halo(part):
        return [
            remote(
                staged_part(part), part_of(2 * side, part),
                row_send.at[part, side], row_recv.at[part, side], frame, me,
            )
            for side, frame in enumerate((later, earlier))
        ]

    def to_sibling(f, part):
        return remote(
            staged_part(part) if f == 1 else part_of(f, part), part_of(f, part),
            side_send.at[f, part], side_recv.at[f, part], seq, sibling,
        )

    def own_row():
        rows = pl.ds(row_base, row_heads)
        return [
            pltpu.make_async_copy(kv_stage.at[rows], kv_row.at[1, column], row_sem.at[0]),
            pltpu.make_async_copy(q_stage.at[rows], q_row, row_sem.at[1]),
        ]

    def start_wide_kv(s, carry):
        send_kv(s, wide_tile)
        return carry

    def start_q(s, carry):
        send_q(s)
        return carry

    def start_near(s, carry):
        send_kv(s, near_tile)
        send_q(s)
        return carry

    def forward(s, carry):
        bytes_of(kv_wide.at[s, 1, pl.ds(0, TILES - 1)], kv_recv.at[s]).wait()
        own_kv(s, wide_tile).wait()
        for copy in halo_copies(s):
            copy.start()
        return carry

    send_kv(0, wide_tile)
    if row_heads:
        for copy in row_halo(0):
            copy.start()
    lax.fori_loop(1, wide, start_wide_kv, 0)
    for part in range(row_parts):
        to_sibling(1, part).start()
    if row_heads:
        for copy in own_row():
            copy.start()
    lax.fori_loop(0, wide, start_q, 0)
    if full > wide:
        lax.fori_loop(wide, full, start_near, 0)
    if half:
        send_half(full)
    lax.fori_loop(0, 2, forward, 0)
    if row_heads:
        for side, copy in enumerate(row_halo(0)):
            copy.wait_recv()
            to_sibling(2 * side, 0).start()
    lax.fori_loop(2, wide, forward, 0)
    if reach_parts > 1:
        for copy in row_halo(1):
            copy.start()

    def row_pairs(part, frames):
        def heads(i, carry):
            for j in range(2):
                head = part * HALF + i * 2 + j
                o_row[head] = attend_row(q_row[head], kv_row, frames, head, table)
            return carry

        lax.fori_loop(0, HALF // 2, heads, 0)

    def row_part(part, frames):
        for f in frames:
            to_sibling(f, part).wait_recv()
        row_pairs(part, frames)

    if row_heads:
        for copy in own_row():
            copy.wait()
        row_part(0, (0, 1, 2))
    for part in range(2, row_parts):
        row_part(part, (1,))

    def attend_slot(s, kv_ref, first_frame):
        bytes_of(q_near.at[s, pl.ds(0, TILES - 1)], q_recv.at[s]).wait()
        own_q(s).wait()

        def write(t, tile):
            o_stage[s, t] = tile

        attend(q_near.at[s], kv_ref, (scores_a, scores_b), write, table, s, first_frame)
        position = s * TILES + spot
        for d in range(1, TILES):
            group = peer(d)
            remote(
                o_stage.at[s, group], out.at[position], o_send.at[s], o_recv.at[s], seq, group
            ).start()
        pltpu.make_async_copy(o_stage.at[s, me], out.at[position], own_sem.at[2, s]).start()

    def wide_slot(s, carry):
        for copy in halo_copies(s):
            copy.wait_recv()
        attend_slot(s, kv_wide.at[s], 0)
        return carry

    def near_slot(s, carry):
        bytes_of(kv_near.at[s - wide, 0, pl.ds(0, TILES - 1)], kv_recv.at[s]).wait()
        own_kv(s, near_tile).wait()
        attend_slot(s, kv_near.at[s - wide], 1)
        return carry

    near = slots - wide
    first = max(wide - near, 0)

    def pair(j, carry):
        if half:
            @pl.when((wide + j < full) | (column == 0))
            def _():
                near_slot(wide + j, 0)
        else:
            near_slot(wide + j, 0)
        wide_slot(first + j, 0)
        return carry

    if first:
        lax.fori_loop(0, first, wide_slot, 0)
    if near:
        lax.fori_loop(0, near, pair, 0)

    if reach_parts > 1:
        for side, copy in enumerate(row_halo(1)):
            copy.wait_recv()
            to_sibling(2 * side, 1).start()
        row_part(1, (0, 1, 2))
    if row_heads:
        pltpu.make_async_copy(o_row, out.at[pl.ds(row_base, row_heads)], row_sem.at[2]).start()

    def own_out(s):
        return pltpu.make_async_copy(o_stage.at[s, me], out.at[s * TILES + spot], own_sem.at[2, s])

    def sent_inputs(s, count):
        bytes_of(kv_stage.at[pl.ds(s * TILES, count)], kv_send.at[s]).wait()
        bytes_of(q_stage.at[pl.ds(s * TILES, count)], q_send.at[s]).wait()

    def got_outputs(s, count):
        bytes_of(out.at[pl.ds(s * TILES, count)], o_recv.at[s]).wait()

    def sent_outputs(s):
        own_out(s).wait()
        bytes_of(o_stage.at[s, pl.ds(0, TILES - 1)], o_send.at[s]).wait()

    def finish(s, carry):
        sent_inputs(s, TILES - 1)
        sent_outputs(s)
        got_outputs(s, TILES - 1)
        return carry

    def finish_halo(s, carry):
        for copy in halo_copies(s):
            copy.wait_send()
        return carry

    lax.fori_loop(0, wide, finish_halo, 0)
    for part in range(reach_parts):
        for copy in row_halo(part):
            copy.wait_send()
    for part in range(row_parts):
        for f in (0, 1, 2) if part < 2 else (1,):
            to_sibling(f, part).wait_send()
    if row_heads:
        pltpu.make_async_copy(o_row, out.at[pl.ds(row_base, row_heads)], row_sem.at[2]).wait()
    if half:
        @pl.when(column == 0)
        def _():
            sent_inputs(full, HALF - 1)
            sent_outputs(full)
            got_outputs(full, HALF - 1)

        @pl.when(column == 1)
        def _():
            sent_inputs(full, HALF)
            got_outputs(full, HALF)
    lax.fori_loop(0, full, finish, 0)


def exchange(halves, wide, collective_id, frame_total, table, kv_stage, q_stage):
    slots = (halves + 1) // 2
    near = max(slots - wide, 1)
    row_heads = max(H - halves * HALF, 1)
    vmem = pl.BlockSpec(memory_space=pltpu.VMEM)
    bf16 = jnp.bfloat16
    tile = (TILE, HD)
    dma = pltpu.SemaphoreType.DMA
    scores = pltpu.VMEM((FRAMES * TILES * TILE, WT * TILE), jnp.float32)
    return pl.pallas_call(
        functools.partial(exchange_kernel, halves, wide, frame_total),
        out_shape=pltpu.VMEM((H,) + tile, bf16),
        in_specs=[pl.BlockSpec(memory_space=pltpu.SMEM), vmem, vmem],
        out_specs=vmem,
        scratch_shapes=[
            pltpu.VMEM((wide, FRAMES, TILES, 2) + tile, bf16),
            pltpu.VMEM((near, 1, TILES, 2) + tile, bf16),
            pltpu.VMEM((FRAMES, WT, row_heads, 2) + tile, bf16),
            pltpu.VMEM((slots, TILES) + tile, bf16),
            pltpu.VMEM((row_heads,) + tile, bf16),
            pltpu.VMEM((slots, TILES) + tile, bf16),
            pltpu.VMEM((row_heads,) + tile, bf16),
            scores, scores,
            dma((slots,)), dma((slots,)), dma((slots,)), dma((slots,)),
            dma((wide, 2)), dma((wide, 2)),
            dma((slots,)), dma((slots,)), dma((3, slots)),
            dma((2, 2)), dma((2, 2)),
            dma((FRAMES, ROW_HEADS // HALF)), dma((FRAMES, ROW_HEADS // HALF)),
            dma((3,)),
        ],
        compiler_params=pltpu.CompilerParams(
            collective_id=collective_id, has_side_effects=True, vmem_limit_bytes=40 << 20
        ),
        name=f"exchange_{halves}_{wide}",
    )(table, kv_stage, q_stage)


def power(exponent):
    return jnp.where(exponent > 0, 2.0, jnp.where(exponent < 0, 0.5, 1.0)).astype(jnp.float32)


def prepare_kernel(
    frame_total,
    extents_hbm, q_exp_hbm, k_exp_hbm, v_exp_hbm, q_data, k_data, v_data,
    table, place, plan, kv_stage, q_stage,
    extents, q_exp, k_exp, v_exp, order, q_in, k_in, v_in, in_sem, small_sem,
):
    loads = [
        pltpu.make_async_copy(src, dst, in_sem.at[i])
        for i, (src, dst) in enumerate(((k_data, k_in), (v_data, v_in), (q_data, q_in)))
    ]
    small = [
        pltpu.make_async_copy(src, dst, small_sem.at[i])
        for i, (src, dst) in enumerate(
            (
                (extents_hbm, extents),
                (k_exp_hbm, k_exp),
                (v_exp_hbm, v_exp),
                (q_exp_hbm, q_exp),
            )
        )
    ]
    for load in small + loads:
        load.start()
    for load in small:
        load.wait()

    zero = jnp.int32(0)
    one = jnp.int32(1)

    def flag(condition):
        return jnp.where(condition, one, zero)

    reach = [flag(extents[0, h] >= 1) for h in range(H)]
    flat = [flag(extents[1, h] <= 0) for h in range(H)]
    reaching = sum(reach, zero)
    flat_reaching = sum((r * f for r, f in zip(reach, flat)), zero)
    row_reaching = jnp.minimum(flat_reaching, ROW_REACH)
    row_most = row_reaching + sum(flat, zero) - flat_reaching
    row_count = zero
    for count in range(HALF, ROW_HEADS + 1, HALF):
        fits = reaching - jnp.minimum(row_reaching, count) <= PLANS[0][1] * TILES
        row_count = jnp.where(fits & (row_most >= count), count, row_count)
    row_reaching = jnp.minimum(row_reaching, row_count)
    row_base = H - row_count
    plan[0] = len(PLANS) - 1 - row_count // HALF
    next_reach, next_rest = zero, reaching - row_reaching
    next_row_reach, next_row_rest = zero, row_reaching
    for h in range(H):
        row_index = jnp.where(reach[h] > 0, next_row_reach, next_row_rest)
        row_end = jnp.where(reach[h] > 0, row_reaching, row_count)
        in_row = flat[h] * flag(row_index < row_end)
        outside = 1 - in_row
        other = jnp.where(reach[h] > 0, next_reach, next_rest)
        position = jnp.where(in_row > 0, row_base + row_index, other)
        next_row_reach += in_row * reach[h]
        next_row_rest += in_row * (1 - reach[h])
        next_reach += outside * reach[h]
        next_rest += outside * (1 - reach[h])
        order[position] = h
        place[h] = position
    me = lax.axis_index("head")
    seq = lax.axis_index("seq")
    column = lax.rem(me, WT)
    spot = column * HALF + me // WT

    def within(condition):
        return jnp.where(condition, 0.0, NEG).astype(jnp.float32)

    def beside(head, f):
        inside = (seq + f - 1 >= 0) & (seq + f - 1 < frame_total)
        return within((extents[0, head] >= abs(f - 1)) & inside)

    for s in range(SLOTS):
        head = order[s * TILES + spot]
        entry = s * ENTRIES
        for r in range(HT):
            for t in range(HT):
                table[entry + r * HT + t] = within(extents[1, head] >= abs(r - t))
        for c in range(WT):
            table[entry + HT * HT + c] = within(extents[2, head] >= c)
        for f in range(FRAMES):
            table[entry + HT * HT + WT + f] = beside(head, f)
    for i in range(ROW_HEADS):
        head = order[jnp.minimum(row_base + i, H - 1)]
        entry = ROW_TABLE + i * ROW_ENTRIES
        for c in range(WT):
            table[entry + c] = within(extents[2, head] >= jnp.abs(column - c))
        for f in range(FRAMES):
            table[entry + WT + f] = beside(head, f)


    def scaled(ref, exps, head):
        columns = pl.ds(pl.multiple_of(head * HD, HD), HD)
        return (ref[:, columns].astype(jnp.float32) * power(exps[0, head])).astype(jnp.bfloat16)

    def stage_keys(s, carry):
        for p in range(TILES):
            kv_stage[s * TILES + p, 0] = scaled(k_in, k_exp, order[s * TILES + p])
        return carry

    def stage_values(s, carry):
        for p in range(TILES):
            kv_stage[s * TILES + p, 1] = scaled(v_in, v_exp, order[s * TILES + p]).T
        return carry

    def stage_queries(s, carry):
        for p in range(TILES):
            q_stage[s * TILES + p] = scaled(q_in, q_exp, order[s * TILES + p])
        return carry

    for load, stage in zip(loads, (stage_keys, stage_values, stage_queries)):
        load.wait()
        lax.fori_loop(0, SLOTS, stage, 0)


def prepare(frame_total, extents, q_exp, k_exp, v_exp, q_data, k_data, v_data):
    smem = pl.BlockSpec(memory_space=pltpu.SMEM)
    bf16 = jnp.bfloat16
    kv = (H, 2, TILE, HD)
    q = (H, TILE, HD)
    vmem = pl.BlockSpec(memory_space=pltpu.VMEM)
    whole = pltpu.VMEM((TILE, H * HD), bf16)
    exponents = pltpu.SMEM((1, H), jnp.int32)
    return pl.pallas_call(
        functools.partial(prepare_kernel, frame_total),
        out_shape=(
            pltpu.SMEM((TABLE,), jnp.float32),
            pltpu.SMEM((H,), jnp.int32),
            pltpu.SMEM((1,), jnp.int32),
            pltpu.VMEM(kv, bf16),
            pltpu.VMEM(q, bf16),
        ),
        in_specs=[pl.BlockSpec(memory_space=pltpu.HBM)] * 7,
        out_specs=(smem, smem, smem, vmem, vmem),
        scratch_shapes=[
            pltpu.SMEM((3, H), jnp.int32),
            exponents, exponents, exponents,
            pltpu.SMEM((H,), jnp.int32),
            whole, whole, whole,
            pltpu.SemaphoreType.DMA((3,)),
            pltpu.SemaphoreType.DMA((4,)),
        ],
        compiler_params=pltpu.CompilerParams(vmem_limit_bytes=58 << 20),
        name="prepare",
    )(extents, q_exp, k_exp, v_exp, q_data, k_data, v_data)


def restore_kernel(place, tiles, out, sem):
    for h in range(H):
        pltpu.make_async_copy(tiles.at[place[h]], out.at[:, pl.ds(h * HD, HD)], sem).start()
    bytes_of(out, sem).wait()


def restore(place, tiles):
    return pl.pallas_call(
        restore_kernel,
        out_shape=pltpu.HBM((TILE, H * HD), jnp.bfloat16),
        in_specs=[
            pl.BlockSpec(memory_space=pltpu.SMEM),
            pl.BlockSpec(memory_space=pltpu.VMEM),
        ],
        out_specs=pl.BlockSpec(memory_space=pl.ANY),
        scratch_shapes=[pltpu.SemaphoreType.DMA(())],
        compiler_params=pltpu.CompilerParams(vmem_limit_bytes=40 << 20),
        name="restore",
    )(place, tiles)


def on_device(frame_total, q_data, k_data, v_data, q_exp, k_exp, v_exp, extents):
    table, place, plan, kv_stage, q_stage = prepare(
        frame_total, extents.T, q_exp, k_exp, v_exp, q_data, k_data, v_data
    )

    def branch(index, halves, wide):
        def run(table, place, kv_stage, q_stage):
            tiles = exchange(halves, wide, index, frame_total, table, kv_stage, q_stage)
            return restore(place, tiles)

        return run

    branches = [branch(i, *plan_sizes) for i, plan_sizes in enumerate(PLANS)]
    return lax.switch(plan[0], branches, table, place, kv_stage, q_stage)


def solution(mesh):
    rows = P(("seq", "head"), None)
    return jax.shard_map(
        functools.partial(on_device, mesh.shape["seq"]),
        mesh=mesh,
        in_specs=(rows,) * 6 + (P(),),
        out_specs=rows,
        check_vma=False,
    )
```

profile of v0, /device:TPU:1, one launch (start us, length us, event | category | flops | bytes accessed | tf_op | source)
XLA Modules:
  0.0 70.4 jit_solution(14514545047739284603)
XLA Ops:
  0.0 3.7 %prepare.1 = (f32[186]{0:T(256)S(4)}, s32[48]{0:T(128)S(4)}, s32[1]{0:T(128)S(4)}, bf16[48,2,128,128]{3,2,1,0:T(8,128)(2,1)S(1)}, bf16[48,128,128]{2,1,0:T(8,128)(2,1)S(1)}) custom-call(s32[3,48]{1,0:T(4,128)} %bitcast.2, s32[1,48]{1,0:T(1,128)} %q_exp_hbm.1, s32[1,48]{1,0:T(1,128)} %k_exp_hbm.1, s32[1,48]{1,0:T(1,128)} %v_exp_hbm.1, ...), custom_call_target="tpu_custom_call" | custom-call | tf_op jit(solution)/shard_map/prepare/pallas_call | solution.py:590
  3.7 66.5 %conditional.1 = (bf16[128,6144]{1,0:T(8,128)(2,1)}) conditional(s32[]{:T(128)} %bitcast.1, (f32[186]{0:T(256)S(4)}, bf16[48,2,128,128]{3,2,1,0:T(8,128)(2,1)S(1)}, bf16[48,128,128]{2,1,0:T(8,128)(2,1)S(1)}, s32[48]{0:T(128)S(4)}) %tuple.17, (f32[186]{0:T(256)S(4)}, bf16[48,2,128,128]{3,2,1,0:T(8,128)(2,1)S(1)}, ...), branch_computations={%region_0.0_spmd, %region_1.0_spmd, %region_2.0_spmd, %region_3.0_... | conditional | bytes 8 | solution.py:648
  3.7 65.0 %exchange_9_3.1.tiles = bf16[48,128,128]{2,1,0:T(8,128)(2,1)S(1)} custom-call(f32[186]{0:T(256)S(4)} %get-tuple-element.42.table, bf16[48,2,128,128]{3,2,1,0:T(8,128)(2,1)S(1)} %get-tuple-element.44.kv_stage, bf16[48,128,128]{2,1,0:T(8,128)(2,1)S(1)} %get-tuple-element.45.q_stage), custom_call_target="tpu_custom_call" | custom-call | tf_op jit(solution)/shard_map/cond/branch_0_fun/exchange_9_3/pallas_call | solution.py:435
  68.7 1.1 %restore.4 = bf16[128,6144]{1,0:T(8,128)(2,1)} custom-call(s32[48]{0:T(128)S(4)} %get-tuple-element.40.place, bf16[48,128,128]{2,1,0:T(8,128)(2,1)S(1)} %exchange_9_3.1.tiles), custom_call_target="tpu_custom_call" | custom-call | tf_op jit(solution)/shard_map/cond/branch_0_fun/restore/pallas_call | solution.py:621
where the time goes:
time: 70.5 us; the launch traced here: 70.4 us
  Pallas kernels  69.8 us (99%)
    pallas_call x1, Pallas kernels, exchange(): pl.pallas_call(functools.partial(exchange_kernel, halves, wide, frame_tot...  65 us
    pallas_call x1, Pallas kernels, prepare(): pl.pallas_call(functools.partial(prepare_kernel, frame_total), out_shape=...  3.68 us

commit v1 on v0

--- a/solution.py
+++ b/solution.py
@@ -39,7 +39,7 @@
     return jnp.max(s.reshape(s.shape[0] // 8, 8, s.shape[1]), axis=0)
 
 
-def attend(q_ref, kv_ref, score_refs, write, table, slot, first_frame):
+def attend(q_ref, kv_ref, score_refs, write, send, table, slot, first_frame):
     frames = kv_ref.shape[0]
     entry = slot * ENTRIES
 
@@ -97,6 +97,9 @@
         peaks = [score(r, s_ref) for r, s_ref in zip(at, score_refs)]
         for r, s_ref, peak in zip(at, score_refs, peaks):
             combine(r, s_ref, peak)
+        for r in at:
+            for u in range(WT):
+                send(r * WT + u)
         return carry
 
     lax.fori_loop(0, HT // 2, rows, 0)
@@ -328,14 +331,20 @@
         def write(t, tile):
             o_stage[s, t] = tile
 
-        attend(q_near.at[s], kv_ref, (scores_a, scores_b), write, table, s, first_frame)
         position = s * TILES + spot
-        for d in range(1, TILES):
-            group = peer(d)
-            remote(
-                o_stage.at[s, group], out.at[position], o_send.at[s], o_recv.at[s], seq, group
-            ).start()
-        pltpu.make_async_copy(o_stage.at[s, me], out.at[position], own_sem.at[2, s]).start()
+
+        def send(t):
+            @pl.when(t == me)
+            def _():
+                pltpu.make_async_copy(o_stage.at[s, t], out.at[position], own_sem.at[2, s]).start()
+
+            @pl.when(t != me)
+            def _():
+                remote(
+                    o_stage.at[s, t], out.at[position], o_send.at[s], o_recv.at[s], seq, t
+                ).start()
+
+        attend(q_near.at[s], kv_ref, (scores_a, scores_b), write, send, table, s, first_frame)
 
     def wide_slot(s, carry):
         for copy in halo_copies(s):

time: 70.5 us -> 74.8 us (1.061)
  Pallas kernels: 69.8 us -> 74.1 us
    pallas_call x1, Pallas kernels: 65 us -> 69.3 us  [exchange(): pl.pallas_call(functools.partial(exchange_kernel, halves, wide, frame_tot...]
where the time goes in v1:
time: 74.8 us
  Pallas kernels  74.1 us (99%)
    pallas_call x1, Pallas kernels, exchange(): pl.pallas_call(functools.partial(exchange_kernel, halves, wide, frame_tot...  69.3 us
    pallas_call x1, Pallas kernels, prepare(): pl.pallas_call(functools.partial(prepare_kernel, frame_total), out_shape=...  3.68 us

profile of v1, /device:TPU:1, one launch (start us, length us, event | category | flops | bytes accessed | tf_op | source)
XLA Modules:
  0.0 74.8 jit_solution(3324665460827628308)
XLA Ops:
  0.0 3.7 %prepare.1 = (f32[186]{0:T(256)S(4)}, s32[48]{0:T(128)S(4)}, s32[1]{0:T(128)S(4)}, bf16[48,2,128,128]{3,2,1,0:T(8,128)(2,1)S(1)}, bf16[48,128,128]{2,1,0:T(8,128)(2,1)S(1)}) custom-call(s32[3,48]{1,0:T(4,128)} %bitcast.2, s32[1,48]{1,0:T(1,128)} %q_exp_hbm.1, s32[1,48]{1,0:T(1,128)} %k_exp_hbm.1, s32[1,48]{1,0:T(1,128)} %v_exp_hbm.1, ...), custom_call_target="tpu_custom_call" | custom-call | tf_op jit(solution)/shard_map/prepare/pallas_call | solution.py:599
  3.7 70.9 %conditional.1 = (bf16[128,6144]{1,0:T(8,128)(2,1)}) conditional(s32[]{:T(128)} %bitcast.1, (f32[186]{0:T(256)S(4)}, bf16[48,2,128,128]{3,2,1,0:T(8,128)(2,1)S(1)}, bf16[48,128,128]{2,1,0:T(8,128)(2,1)S(1)}, s32[48]{0:T(128)S(4)}) %tuple.17, (f32[186]{0:T(256)S(4)}, bf16[48,2,128,128]{3,2,1,0:T(8,128)(2,1)S(1)}, ...), branch_computations={%region_0.0_spmd, %region_1.0_spmd, %region_2.0_spmd, %region_3.0_... | conditional | bytes 8 | solution.py:657
  3.9 69.3 %exchange_10_3.1.tiles = bf16[48,128,128]{2,1,0:T(8,128)(2,1)S(1)} custom-call(f32[186]{0:T(256)S(4)} %get-tuple-element.47.table, bf16[48,2,128,128]{3,2,1,0:T(8,128)(2,1)S(1)} %get-tuple-element.48.kv_stage, bf16[48,128,128]{2,1,0:T(8,128)(2,1)S(1)} %get-tuple-element.49.q_stage), custom_call_target="tpu_custom_call" | custom-call | tf_op jit(solution)/shard_map/cond/branch_1_fun/exchange_10_3/pallas_call | solution.py:444
  73.2 1.1 %restore.5 = bf16[128,6144]{1,0:T(8,128)(2,1)} custom-call(s32[48]{0:T(128)S(4)} %get-tuple-element.46.place, bf16[48,128,128]{2,1,0:T(8,128)(2,1)S(1)} %exchange_10_3.1.tiles), custom_call_target="tpu_custom_call" | custom-call | tf_op jit(solution)/shard_map/cond/branch_1_fun/restore/pallas_call | solution.py:630

commit v2 on v1

--- a/solution.py
+++ b/solution.py
@@ -176,14 +176,14 @@
         remote(src, tile_at(s, me), kv_send.at[s], kv_recv.at[s], seq, group).start()
 
     def send_q_tile(s, place, group):
-        src = q_stage.at[s * TILES + place]
+        src = q_stage.at[s, place]
         remote(src, q_near.at[s, me], q_send.at[s], q_recv.at[s], seq, group).start()
 
     def own_kv(s, tile_at):
         return pltpu.make_async_copy(kv_stage.at[s * TILES + spot], tile_at(s, me), own_sem.at[0, s])
 
     def own_q(s):
-        return pltpu.make_async_copy(q_stage.at[s * TILES + spot], q_near.at[s, me], own_sem.at[1, s])
+        return pltpu.make_async_copy(q_stage.at[s, spot], q_near.at[s, me], own_sem.at[1, s])
 
     def place_of(group):
         return lax.rem(group, WT) * HALF + group // WT
@@ -253,17 +253,27 @@
 
     def own_row():
         rows = pl.ds(row_base, row_heads)
-        return [
-            pltpu.make_async_copy(kv_stage.at[rows], kv_row.at[1, column], row_sem.at[0]),
-            pltpu.make_async_copy(q_stage.at[rows], q_row, row_sem.at[1]),
-        ]
+        return pltpu.make_async_copy(kv_stage.at[rows], kv_row.at[1, column], row_sem.at[0])
+
+    def own_row_q(part):
+        slot, start = divmod(row_base + part * HALF, TILES)
+        src = q_stage.at[slot, pl.ds(start, HALF)]
+        return pltpu.make_async_copy(src, q_row.at[pl.ds(part * HALF, HALF)], row_sem.at[1])
+
+    wide_slots = pl.ds(0, wide)
+
+    def send_wide_q():
+        for d in range(1, TILES):
+            group = peer(d)
+            remote(
+                q_stage.at[wide_slots, place_of(group)], q_near.at[wide_slots, me],
+                q_send.at[0], q_recv.at[0], seq, group,
+            ).start()
+        for s in range(wide):
+            own_q(s).start()
 
     def start_wide_kv(s, carry):
         send_kv(s, wide_tile)
-        return carry
-
-    def start_q(s, carry):
-        send_q(s)
         return carry
 
     def start_near(s, carry):
@@ -286,9 +296,10 @@
     for part in range(row_parts):
         to_sibling(1, part).start()
     if row_heads:
-        for copy in own_row():
-            copy.start()
-    lax.fori_loop(0, wide, start_q, 0)
+        own_row().start()
+        for part in range(row_parts):
+            own_row_q(part).start()
+    send_wide_q()
     if full > wide:
         lax.fori_loop(wide, full, start_near, 0)
     if half:
@@ -318,14 +329,13 @@
         row_pairs(part, frames)
 
     if row_heads:
-        for copy in own_row():
-            copy.wait()
+        own_row().wait()
+        bytes_of(q_row, row_sem.at[1]).wait()
         row_part(0, (0, 1, 2))
     for part in range(2, row_parts):
         row_part(part, (1,))
 
     def attend_slot(s, kv_ref, first_frame):
-        bytes_of(q_near.at[s, pl.ds(0, TILES - 1)], q_recv.at[s]).wait()
         own_q(s).wait()
 
         def write(t, tile):
@@ -355,6 +365,7 @@
     def near_slot(s, carry):
         bytes_of(kv_near.at[s - wide, 0, pl.ds(0, TILES - 1)], kv_recv.at[s]).wait()
         own_kv(s, near_tile).wait()
+        bytes_of(q_near.at[s, pl.ds(0, TILES - 1)], q_recv.at[s]).wait()
         attend_slot(s, kv_near.at[s - wide], 1)
         return carry
 
@@ -371,6 +382,7 @@
         wide_slot(first + j, 0)
         return carry
 
+    bytes_of(q_near.at[wide_slots, pl.ds(0, TILES - 1)], q_recv.at[0]).wait()
     if first:
         lax.fori_loop(0, first, wide_slot, 0)
     if near:
@@ -389,7 +401,9 @@
 
     def sent_inputs(s, count):
         bytes_of(kv_stage.at[pl.ds(s * TILES, count)], kv_send.at[s]).wait()
-        bytes_of(q_stage.at[pl.ds(s * TILES, count)], q_send.at[s]).wait()
+
+    def sent_queries(s, count):
+        bytes_of(q_stage.at[s, pl.ds(0, count)], q_send.at[s]).wait()
 
     def got_outputs(s, count):
         bytes_of(out.at[pl.ds(s * TILES, count)], o_recv.at[s]).wait()
@@ -402,6 +416,10 @@
         sent_inputs(s, TILES - 1)
         sent_outputs(s)
         got_outputs(s, TILES - 1)
+        return carry
+
+    def finish_queries(s, carry):
+        sent_queries(s, TILES - 1)
         return carry
 
     def finish_halo(s, carry):
@@ -422,13 +440,18 @@
         @pl.when(column == 0)
         def _():
             sent_inputs(full, HALF - 1)
+            sent_queries(full, HALF - 1)
             sent_outputs(full)
             got_outputs(full, HALF - 1)
 
         @pl.when(column == 1)
         def _():
             sent_inputs(full, HALF)
+            sent_queries(full, HALF)
             got_outputs(full, HALF)
+    bytes_of(q_stage.at[wide_slots, pl.ds(0, TILES - 1)], q_send.at[0]).wait()
+    if full > wide:
+        lax.fori_loop(wide, full, finish_queries, 0)
     lax.fori_loop(0, full, finish, 0)
 
 
@@ -580,7 +603,7 @@
 
     def stage_queries(s, carry):
         for p in range(TILES):
-            q_stage[s * TILES + p] = scaled(q_in, q_exp, order[s * TILES + p])
+            q_stage[s, p] = scaled(q_in, q_exp, order[s * TILES + p])
         return carry
 
     for load, stage in zip(loads, (stage_keys, stage_values, stage_queries)):
@@ -592,7 +615,7 @@
     smem = pl.BlockSpec(memory_space=pltpu.SMEM)
     bf16 = jnp.bfloat16
     kv = (H, 2, TILE, HD)
-    q = (H, TILE, HD)
+    q = (SLOTS, TILES, TILE, HD)
     vmem = pl.BlockSpec(memory_space=pltpu.VMEM)
     whole = pltpu.VMEM((TILE, H * HD), bf16)
     exponents = pltpu.SMEM((1, H), jnp.int32)

time: 74.8 us -> 70 us (0.936)
  Pallas kernels: 74.1 us -> 69.3 us
    pallas_call x1, Pallas kernels: 69.3 us -> 64.5 us  [exchange(): pl.pallas_call(functools.partial(exchange_kernel, halves, wide, frame_tot...]
where the time goes in v2:
time: 70 us; the launch traced here: 69.9 us
  Pallas kernels  69.3 us (99%)
    pallas_call x1, Pallas kernels, exchange(): pl.pallas_call(functools.partial(exchange_kernel, halves, wide, frame_tot...  64.5 us
    pallas_call x1, Pallas kernels, prepare(): pl.pallas_call(functools.partial(prepare_kernel, frame_total), out_shape=...  3.68 us

profile of v2, /device:TPU:1, one launch (start us, length us, event | category | flops | bytes accessed | tf_op | source)
XLA Modules:
  0.0 69.9 jit_solution(6222938833868588443)
XLA Ops:
  0.0 3.7 %prepare.1 = (f32[186]{0:T(256)S(4)}, s32[48]{0:T(128)S(4)}, s32[1]{0:T(128)S(4)}, bf16[48,2,128,128]{3,2,1,0:T(8,128)(2,1)S(1)}, bf16[6,8,128,128]{3,2,1,0:T(8,128)(2,1)S(1)}) custom-call(s32[3,48]{1,0:T(4,128)} %bitcast.2, s32[1,48]{1,0:T(1,128)} %q_exp_hbm.1, s32[1,48]{1,0:T(1,128)} %k_exp_hbm.1, s32[1,48]{1,0:T(1,128)} %v_exp_hbm.1, ...), custom_call_target="tpu_custom_call" | custom-call | tf_op jit(solution)/shard_map/prepare/pallas_call | solution.py:622
  3.7 66.0 %conditional.1 = (bf16[128,6144]{1,0:T(8,128)(2,1)}) conditional(s32[]{:T(128)} %bitcast.1, (f32[186]{0:T(256)S(4)}, bf16[48,2,128,128]{3,2,1,0:T(8,128)(2,1)S(1)}, bf16[6,8,128,128]{3,2,1,0:T(8,128)(2,1)S(1)}, s32[48]{0:T(128)S(4)}) %tuple.17, (f32[186]{0:T(256)S(4)}, bf16[48,2,128,128]{3,2,1,0:T(8,128)(2,1)S(1)}, ...), branch_computations={%region_0.0_spmd, %region_1.0_spmd, %region_2.0_spmd, %region_3.0_... | conditional | bytes 8 | solution.py:680
  3.7 64.5 %exchange_9_3.1.tiles = bf16[48,128,128]{2,1,0:T(8,128)(2,1)S(1)} custom-call(f32[186]{0:T(256)S(4)} %get-tuple-element.42.table, bf16[48,2,128,128]{3,2,1,0:T(8,128)(2,1)S(1)} %get-tuple-element.44.kv_stage, bf16[6,8,128,128]{3,2,1,0:T(8,128)(2,1)S(1)} %get-tuple-element.45.q_stage), custom_call_target="tpu_custom_call" | custom-call | tf_op jit(solution)/shard_map/cond/branch_0_fun/exchange_9_3/pallas_call | solution.py:467
  68.2 1.1 %restore.4 = bf16[128,6144]{1,0:T(8,128)(2,1)} custom-call(s32[48]{0:T(128)S(4)} %get-tuple-element.40.place, bf16[48,128,128]{2,1,0:T(8,128)(2,1)S(1)} %exchange_9_3.1.tiles), custom_call_target="tpu_custom_call" | custom-call | tf_op jit(solution)/shard_map/cond/branch_0_fun/restore/pallas_call | solution.py:653
